TPU v7x, 32 devices: a whole 2x2x4 slice. The times are simulated.
32 devices in a mesh: tm: 4 (over x, core), mic: 8 (over z, y).
Axes of the slice: x: 2, y: 2, z: 4, core: 2. Of those that a mesh axis runs over, the one named last changes fastest.
Arguments:
- samples: bfloat16 [32, 4096, 4096], P('tm', 'mic'), may hold values from -6 to 6
- bin_ids: int32 [16], replicated, may hold values from 1 to 2047
- delays: int32 [1024, 4096], P('mic'), may hold values from 0 to 1023
Outputs:
- source_map: float32 [16, 1024], P('tm', 'mic')
All inputs are finite; a program needn't handle non-finite values.
Results may differ from a plain program's by a relative error of at most 0.0013.
Values may be sent and summed in bfloat16 or wider, within the bound.
A program may use at most 64 MiB of HBM per device.

v0:
```python
import math

import jax
import jax.numpy as jnp
from jax import lax
from jax.sharding import PartitionSpec as P


def dft_table(bin_ids, length):
    sample_index = jnp.arange(length, dtype=jnp.int32)
    window = 0.5 - 0.5 * jnp.cos(2.0 * jnp.pi * sample_index.astype(jnp.float32) / length)
    window_norm = jnp.sqrt(jnp.sum(window * window))
    phase_index = sample_index[:, None] * bin_ids[None, :] % length
    angles = 2.0 * jnp.pi * phase_index.astype(jnp.float32) / length
    cosine = window[:, None] * jnp.cos(angles) / window_norm
    sine_part = -window[:, None] * jnp.sin(angles) / window_norm
    return jnp.stack([cosine, sine_part], axis=-1).reshape(length, -1).astype(jnp.bfloat16)


def steer_block(received, delay_cols, bins_owned, length):
    seg_count = received.shape[0]
    mic_count = received.shape[3]
    point_count = delay_cols.shape[0]

    def per_bin(entry):
        bin_value, values = entry
        phases = 2.0 * jnp.pi * (bin_value * delay_cols % length).astype(jnp.float32) / length
        steer_rows = jnp.concatenate([jnp.cos(phases), jnp.sin(phases)], axis=0).astype(
            jnp.bfloat16
        )
        product = lax.dot_general(
            values.reshape(seg_count * 2, mic_count),
            steer_rows,
            (((1,), (1,)), ((), ())),
            preferred_element_type=jnp.float32,
        )
        product = product.reshape(seg_count, 2, 2, point_count)
        real_part = product[:, 0, 0] - product[:, 1, 1]
        imag_part = product[:, 1, 0] + product[:, 0, 1]
        return jnp.stack([real_part, imag_part], axis=0)

    return lax.map(per_bin, (bins_owned, jnp.moveaxis(received, 1, 0)))


def per_device(samples, bin_ids, delays):
    length = samples.shape[2]
    transform_rows = dft_table(bin_ids, length)
    spectra = jnp.einsum("sml,lk->skm", samples, transform_rows, preferred_element_type=jnp.float32)
    spectra = spectra.reshape(samples.shape[0], bin_ids.shape[0], 2, samples.shape[1]).astype(
        jnp.bfloat16
    )
    spectra = lax.all_to_all(spectra, "tm", split_axis=1, concat_axis=0, tiled=True)
    bin_share = spectra.shape[1]
    bins_owned = lax.dynamic_slice_in_dim(bin_ids, lax.axis_index("tm") * bin_share, bin_share)
    seg_count = spectra.shape[0]
    bin_share = spectra.shape[1]
    steered = steer_block(
        lax.all_gather(spectra, "mic", axis=3, tiled=True), delays, bins_owned, length
    )
    steered = steered / math.sqrt(delays.shape[1])
    powers = jnp.sum(steered * steered, axis=(1, 2))
    return powers / seg_count


def solution(mesh):
    placed = (P("tm", "mic", None), P(), P("mic", None))
    return jax.shard_map(
        per_device, mesh=mesh, in_specs=placed, out_specs=P("tm", "mic"), check_vma=False
    )
```

profile of v0, /device:TPU:0, one launch (start us, length us, event | category | flops | bytes accessed | tf_op | source)
XLA Modules:
  0.0 142.6 jit_solution(10239298396798844468)
XLA Ops:
  6.5 0.0 all-gather.2.cloned.1.call-start
  6.5 0.1 multiply_subtract_fusion
  6.6 0.7 multiply_reduce_fusion.1
  8.0 1.9 %divide_convert_fusion.1 = (bf16[4096,16,1]{0,1,2:T(8,128)(2,1)S(1)}, bf16[4096,16,1]{0,1,2:T(8,128)(2,1)S(1)}) fusion(f32[]{:T(128)S(6)} %sqrt.3, s32[16]{0:T(128)} %param.6, f32[4096]{0:T(1024)S(1)} %get-tuple-element.89, f32[4096]{0:T(1024)S(1)} %get-tuple-element.90), kind=kLoop, calls=%fused_computation.30 | loop fusion | flops 1310720 | bytes 294980 | tf_op jit(solution)/shard_map/convert.2
  9.9 0.3 copy.9
  10.2 0.1 reshape.233
  10.3 15.3 %fusion.10 = bf16[8,32,512]{2,1,0:T(8,128)(2,1)S(1)} fusion(bf16[4096,32,1]{0,1,2:T(8,128)(2,1)S(1)} %reshape.233, bf16[8,512,4096]{2,1,0:T(8,128)(2,1)} %param.5), kind=kOutput, calls=%fused_computation.20 | convolution fusion | flops 1073872896 | bytes 34078720 | tf_op jit(solution)/shard_map/sml,lk->skm/dot_general | solution.py:48
  25.6 0.0 copy-start.1
  25.6 0.0 copy-start
  25.6 0.1 convert_element_type.66
  25.7 0.2 copy.10
  26.0 10.2 %all_to_all.18 = bf16[8,16,2,512]{3,2,0,1:T(2,128)(2,1)S(1)} all-to-all(bf16[8,16,2,512]{3,2,0,1:T(2,128)(2,1)S(1)} %copy.10), channel_id=1, replica_groups=mesh['tm'=4,'mic'=8] {'tm'}, dimensions={1} | all-to-all | bytes 524288 | tf_op jit(solution)/shard_map/all_to_all | solution.py:52
  36.2 0.7 copy.14
  36.9 0.0 all-gather.2.cloned.1.call-update
  36.9 0.0 copy-done.1
  36.9 0.1 dynamic_slice.17
  37.0 51.4 %all-gather.2.cloned.1.call-done = bf16[32,4,2,4096]{3,0,2,1:T(8,128)(2,1)} async-done(((bf16[32,4,2,512]{3,0,2,1:T(8,128)(2,1)}), bf16[32,4,2,4096]{3,0,2,1:T(8,128)(2,1)}) %all-gather.2.cloned.1.call-update) | async-done | bytes 2097168 | tf_op jit(solution)/shard_map/all_gather | solution.py:58
  88.5 0.0 copy-done
  88.5 46.7 %while.12 = (s32[]{:T(128)}, f32[4,2,32,128]{3,2,1,0:T(8,128)S(1)}, bf16[4,32,2,4096]{3,1,2,0:T(8,128)(2,1)}, s32[4]{0:T(128)S(1)}, s32[128,4096]{1,0:T(8,128)S(1)}, /*index=5*/s32[]{:T(128)}) while((s32[]{:T(128)}, f32[4,2,32,128]{3,2,1,0:T(8,128)S(1)}, bf16[4,32,2,4096]{3,1,2,0:T(8,128)(2,1)}, s32[4]{0:T(128)S(1)}, ...), condition=%wide.region_2.3_spmd, body=%wide.region_1.2_spmd.sunk | while | flops 146817024 | bytes 11240025 | solution.py:42
  88.5 0.6 dynamic_slice.25
  89.1 9.0 %cosine_convert_fusion.2 = (bf16[128,4096]{1,0:T(8,128)(2,1)S(1)}, bf16[128,4096]{1,0:T(8,128)(2,1)S(1)}) fusion(s32[128,4096]{1,0:T(8,128)S(1)} %get-tuple-element.146, s32[]{:T(128)} %bitcast.42), kind=kLoop, calls=%fused_computation.8.clone.1 | loop fusion | flops 8388608 | bytes 4194308 | tf_op jit(solution)/shard_map/convert
  98.1 0.2 pad_maximum_fusion.3
  98.3 1.8 %fusion.28 = f32[32,2,2,128]{3,0,2,1:T(8,128)S(1)} fusion(bf16[2,128,4096,1]{2,1,0,3:T(8,128)(2,1)S(1)} %bitcast.44, bf16[4,32,2,4096]{3,1,2,0:T(8,128)(2,1)} %get-tuple-element.144, s32[]{:T(128)} %get-tuple-element.136), kind=kOutput, calls=%fused_computation.9.clone.1 | convolution fusion | flops 134217728 | bytes 2687488 | tf_op jit(solution)/shard_map/while/body/eval_jaxpr/dot_general | solution.py:31
  100.1 0.6 dynamic_slice.25
  100.7 9.0 %cosine_convert_fusion.2 = (bf16[128,4096]{1,0:T(8,128)(2,1)S(1)}, bf16[128,4096]{1,0:T(8,128)(2,1)S(1)}) fusion(s32[128,4096]{1,0:T(8,128)S(1)} %get-tuple-element.146, s32[]{:T(128)} %bitcast.42), kind=kLoop, calls=%fused_computation.8.clone.1 | loop fusion | flops 8388608 | bytes 4194308 | tf_op jit(solution)/shard_map/convert
  109.8 0.2 pad_maximum_fusion.3
  110.0 1.8 %fusion.28 = f32[32,2,2,128]{3,0,2,1:T(8,128)S(1)} fusion(bf16[2,128,4096,1]{2,1,0,3:T(8,128)(2,1)S(1)} %bitcast.44, bf16[4,32,2,4096]{3,1,2,0:T(8,128)(2,1)} %get-tuple-element.144, s32[]{:T(128)} %get-tuple-element.136), kind=kOutput, calls=%fused_computation.9.clone.1 | convolution fusion | flops 134217728 | bytes 2687488 | tf_op jit(solution)/shard_map/while/body/eval_jaxpr/dot_general | solution.py:31
  111.8 0.6 dynamic_slice.25
  112.4 9.0 %cosine_convert_fusion.2 = (bf16[128,4096]{1,0:T(8,128)(2,1)S(1)}, bf16[128,4096]{1,0:T(8,128)(2,1)S(1)}) fusion(s32[128,4096]{1,0:T(8,128)S(1)} %get-tuple-element.146, s32[]{:T(128)} %bitcast.42), kind=kLoop, calls=%fused_computation.8.clone.1 | loop fusion | flops 8388608 | bytes 4194308 | tf_op jit(solution)/shard_map/convert
  121.4 0.2 pad_maximum_fusion.3
  121.6 1.8 %fusion.28 = f32[32,2,2,128]{3,0,2,1:T(8,128)S(1)} fusion(bf16[2,128,4096,1]{2,1,0,3:T(8,128)(2,1)S(1)} %bitcast.44, bf16[4,32,2,4096]{3,1,2,0:T(8,128)(2,1)} %get-tuple-element.144, s32[]{:T(128)} %get-tuple-element.136), kind=kOutput, calls=%fused_computation.9.clone.1 | convolution fusion | flops 134217728 | bytes 2687488 | tf_op jit(solution)/shard_map/while/body/eval_jaxpr/dot_general | solution.py:31
  123.5 0.6 dynamic_slice.25
  124.1 9.0 %cosine_convert_fusion.2 = (bf16[128,4096]{1,0:T(8,128)(2,1)S(1)}, bf16[128,4096]{1,0:T(8,128)(2,1)S(1)}) fusion(s32[128,4096]{1,0:T(8,128)S(1)} %get-tuple-element.146, s32[]{:T(128)} %bitcast.42), kind=kLoop, calls=%fused_computation.8.clone.1 | loop fusion | flops 8388608 | bytes 4194308 | tf_op jit(solution)/shard_map/convert
  133.1 0.2 pad_maximum_fusion.3
  133.3 1.8 %fusion.28 = f32[32,2,2,128]{3,0,2,1:T(8,128)S(1)} fusion(bf16[2,128,4096,1]{2,1,0,3:T(8,128)(2,1)S(1)} %bitcast.44, bf16[4,32,2,4096]{3,1,2,0:T(8,128)(2,1)} %get-tuple-element.144, s32[]{:T(128)} %get-tuple-element.136), kind=kOutput, calls=%fused_computation.9.clone.1 | convolution fusion | flops 134217728 | bytes 2687488 | tf_op jit(solution)/shard_map/while/body/eval_jaxpr/dot_general | solution.py:31
  135.2 0.6 broadcast_multiply_fusion
  (11 shorter events, 0.1 us)
Async XLA Ops:
  6.5 81.9 %all-gather.2.cloned.1.call-start = ((), (), s32[]{:S(2)}) async-start(), calls=%async_computation.1 | async-start | bytes 2359296 | tf_op jit(solution)/shard_map/all_gather | solution.py:58
  25.6 11.3 %copy-start.1 = (s32[16]{0:T(128)S(1)}, s32[16]{0:T(128)}, u32[]{:S(2)}) copy-start(s32[16]{0:T(128)} %param.6) | copy-start | bytes 196
  25.6 62.9 %copy-start = (s32[128,4096]{1,0:T(8,128)S(1)}, s32[128,4096]{1,0:T(8,128)}, u32[]{:S(2)}) copy-start(s32[128,4096]{1,0:T(8,128)} %param.7) | copy-start | bytes 6291460
Sparse Core Ops, SparseCore 0:
  37.0 51.3 all-gather.1
where the time goes:
time: 143 us
  waiting for transfers between devices  51.5 us (36%)
  other arithmetic  40.2 us (28%)
  matrix products  22.5 us (16%)
  between operations  14.2 us (10%)
  blocking collectives  10.2 us (7%)
  local copies, waits for them, and re-layouts  3.92 us (3%)
    all_gather x1, waiting for transfers between devices, per_device(): lax.all_gather(spectra, 'mic', axis=3, tiled=True)  51.4 us
    another operation x5, other arithmetic  37.9 us
    dot_general x1, matrix products, per_device(): jnp.einsum('sml,lk->skm', samples, transform_rows, preferred_element_type...  15.3 us
    all_to_all x1, blocking collectives, per_device(): lax.all_to_all(spectra, 'tm', split_axis=1, concat_axis=0, tiled=True)  10.2 us
    dot_general x4, matrix products, per_bin(): lax.dot_general(values.reshape(seg_count * 2, mic_count), steer_rows, (((...  7.22 us
  transfers between devices with their start and end apart: 1, of which 1 were waited for; matrix products, arithmetic and copies ran while one was open for 0% of the time, Pallas kernels for 0%

commit v1 on v0

v1 whole, which is shorter than its diff:
```python
import functools
import math

import jax
import jax.numpy as jnp
import numpy as np
from jax import lax
from jax.experimental import pallas as pl
from jax.experimental.pallas import tpu as pltpu
from jax.sharding import PartitionSpec as P

MESH = pl.DeviceIdType.MESH
NT = (((1,), (1,)), ((), ()))


def fit(function, count):
    nodes = 0.125 + 0.125 * np.cos(np.pi * (np.arange(64) + 0.5) / 64)
    series = np.polynomial.chebyshev.Chebyshev.fit(nodes, function(np.sqrt(nodes)), count - 1, domain=[0, 0.25])
    return [float(c) for c in series.convert(kind=np.polynomial.Polynomial).coef]


SIN_HALF = fit(lambda r: np.sin(np.pi * r) / r, 5)
COS_HALF = fit(lambda r: np.cos(np.pi * r), 6)


def horner(coefficients, y):
    total = coefficients[-1]
    for c in coefficients[-2::-1]:
        total = total * y + c
    return total


def fraction(turns):
    return turns - ((turns + 12582912.0) - 12582912.0)


def cos_turns(turns):
    r = fraction(turns)
    s = r * horner(SIN_HALF, r * r)
    return 1.0 - (s + s) * s


def cos_sin_turns(turns):
    r = fraction(turns)
    y = r * r
    s = r * horner(SIN_HALF, y)
    twice = s + s
    return 1.0 - twice * s, twice * horner(COS_HALF, y)


def kernel(dims, bins, samples, delays, out, table, held, delay, spec, gath, steer, acc,
           sample_sem, delay_sem, send_sem, fwd_sem, recv_sem):
    T, Z, Y, bin_count, nb, chunk_segs, chunks, parts, group, slots = dims
    mics_here, length = samples.shape[1], samples.shape[2]
    points, mics = delays.shape
    rows = chunk_segs * 2 * nb
    steps = chunks * parts
    t, m = lax.axis_index("tm"), lax.axis_index("mic")
    z, y = lax.div(m, Y), lax.rem(m, Y)

    def mic_of(z2, y2):
        return z2 * Y + y2

    def fetch(i, slot):
        c, q = lax.div(i, parts), lax.rem(i, parts)
        return pltpu.make_async_copy(
            samples.at[pl.ds(c * chunk_segs, chunk_segs), pl.ds(pl.multiple_of(q * group, group), group)],
            held.at[slot], sample_sem.at[slot])

    for i in range(min(slots, steps)):
        fetch(i, i).start()
        if i == 0:
            pltpu.make_async_copy(delays, delay, delay_sem).start()

    near = [(lax.rem(t + a, T), mic_of(lax.rem(z + k, Z), y)) for k in range(Z) for a in range(T) if k or a]
    across = [(lax.rem(t + a, T), mic_of(z, 1 - y)) for a in range(T)] if Y == 2 else []
    peers = near + across
    barrier = pltpu.get_barrier_semaphore()
    for t2, m2 in peers:
        pl.semaphore_signal(barrier, inc=1, device_id={"tm": t2, "mic": m2}, device_id_type=MESH)

    table_rows = 2 * bin_count
    row = lax.broadcasted_iota(jnp.int32, (table_rows, 128), 0)
    lane = lax.broadcasted_iota(jnp.int32, (table_rows, 128), 1)
    bin_of = (row // (2 * nb)) * nb + row % nb
    scale = jnp.zeros((table_rows, 128), jnp.float32)
    for i in range(bin_count):
        scale = jnp.where(bin_of == i, bins[i].astype(jnp.float32) * (1.0 / length), scale)
    quarter = jnp.where((row // nb) % 2 == 1, jnp.float32(0.25), jnp.float32(0.0))
    lane8 = lax.broadcasted_iota(jnp.int32, (8, 128), 1)

    def window_at(j, like):
        return 0.5 - 0.5 * cos_turns((like + j * 128).astype(jnp.float32) * (1.0 / length))

    def norm_step(j, total):
        w = window_at(j, lane8)
        return total + w * w

    norm = jnp.sum(lax.fori_loop(0, length // 128, norm_step, jnp.zeros((8, 128), jnp.float32), unroll=4),
                   axis=1, keepdims=True)[0:1]
    inverse = 1.0 / jnp.sqrt(norm)

    def table_step(j, carry):
        w = window_at(j, lane8)[0:1] * inverse
        turns = (lane + j * 128).astype(jnp.float32) * scale + quarter
        table[:, pl.ds(pl.multiple_of(j * 128, 128), 128)] = (w * cos_turns(turns)).astype(jnp.bfloat16)
        return carry

    lax.fori_loop(0, length // 128, table_step, 0, unroll=4)

    pltpu.make_async_copy(delays, delay, delay_sem).wait()
    own_scale = [bins[t * nb + b].astype(jnp.float32) * (1.0 / length) for b in range(nb)]
    point_part = points // steps
    width = 512 if mics % 512 == 0 else 128

    def block_rows(c):
        return pl.ds(pl.multiple_of(c * T * rows, T * rows), T * rows)

    def push(c, index, t2, m2):
        return pltpu.make_async_remote_copy(
            src_ref=spec.at[c, pl.ds(pl.multiple_of(t2 * rows, rows), rows)],
            dst_ref=gath.at[m, pl.ds(pl.multiple_of(c * T * rows + t * rows, rows), rows)],
            send_sem=send_sem.at[c, index], recv_sem=recv_sem.at[c, m],
            device_id={"tm": t2, "mic": m2}, device_id_type=MESH)

    def forward(c, k):
        m2 = mic_of(lax.rem(z + k, Z), y)
        return pltpu.make_async_remote_copy(
            src_ref=gath.at[m2, block_rows(c)], dst_ref=gath.at[m2, block_rows(c)],
            send_sem=fwd_sem.at[c, k - 1], recv_sem=recv_sem.at[c, m2],
            device_id={"tm": t, "mic": mic_of(z, 1 - y)}, device_id_type=MESH)

    def arrived(c, m2):
        pltpu.make_async_copy(gath.at[m2, block_rows(c)], gath.at[m2, block_rows(c)], recv_sem.at[c, m2]).wait()

    def send_chunk(c):
        for index, (t2, m2) in enumerate(peers):
            push(c, index, t2, m2).start()
        pltpu.make_async_copy(
            spec.at[c, pl.ds(pl.multiple_of(t * rows, rows), rows)],
            gath.at[m, pl.ds(pl.multiple_of(c * T * rows + t * rows, rows), rows)],
            recv_sem.at[c, m]).start()

    def pass_on(c):
        for k in range(1, Z):
            arrived(c, mic_of(lax.rem(z + k, Z), y))
            if Y == 2:
                forward(c, k).start()

    pl.semaphore_wait(barrier, len(peers))

    def step(i, carry):
        slot = lax.rem(i, slots)
        c, q = lax.div(i, parts), lax.rem(i, parts)
        fetch(i, slot).wait()
        block = held[slot].reshape(chunk_segs * group, length)
        found = lax.dot_general(block, table[...], NT, preferred_element_type=jnp.float32)
        first = pl.multiple_of(i * point_part, point_part)
        for start in range(0, mics, width):
            turns = delay[pl.ds(first, point_part), start:start + width].astype(jnp.float32)
            for b in range(nb):
                cosine, sine = cos_sin_turns(turns * own_scale[b])
                steer[b, 0, pl.ds(first, point_part), start:start + width] = cosine.astype(jnp.bfloat16)
                steer[b, 1, pl.ds(first, point_part), start:start + width] = sine.astype(jnp.bfloat16)
        found = [found[s * group:(s + 1) * group].T for s in range(chunk_segs)]
        for t2 in range(T):
            lines = [f[t2 * 2 * nb:(t2 + 1) * 2 * nb] for f in found]
            spec[c, t2 * rows:(t2 + 1) * rows, pl.ds(pl.multiple_of(q * group, group), group)] = (
                jnp.concatenate(lines, axis=0).astype(jnp.bfloat16))

        @pl.when(i + slots < steps)
        def _():
            fetch(i + slots, slot).start()

        @pl.when(q == parts - 1)
        def _():
            send_chunk(c)

            @pl.when(c >= 1)
            def _():
                pass_on(c - 1)

        return carry

    lax.fori_loop(0, steps, step, 0)
    pass_on(chunks - 1)

    acc[...] = jnp.zeros_like(acc)

    def add_block(m2):
        columns = pl.ds(pl.multiple_of(m2 * mics_here, mics_here), mics_here)
        lhs = steer[:, :, :, columns].reshape(nb * 2 * points, mics_here)
        acc[...] += lax.dot_general(lhs, gath[m2], NT, preferred_element_type=jnp.float32)

    def own_y(k, carry):
        m2 = mic_of(lax.rem(z + k, Z), y)

        @pl.when(k == 0)
        def _():
            for c in range(chunks):
                arrived(c, m2)

        add_block(m2)
        return carry

    lax.fori_loop(0, Z, own_y, 0)

    def other_y(k, carry):
        m2 = mic_of(lax.rem(z + k, Z), 1 - y)
        for c in range(chunks):
            arrived(c, m2)
        add_block(m2)
        return carry

    if Y == 2:
        lax.fori_loop(0, Z, other_y, 0)

    columns = chunks * T * rows
    column = lax.broadcasted_iota(jnp.int32, (points, columns), 1)
    for b in range(nb):
        along_cos = acc[(2 * b) * points:(2 * b + 1) * points]
        along_sin = acc[(2 * b + 1) * points:(2 * b + 2) * points]
        real = along_cos - pltpu.roll(along_sin, columns - nb, axis=1)
        imag = pltpu.roll(along_cos, columns - nb, axis=1) + along_sin
        power = jnp.where(column % (2 * nb) == b, real * real + imag * imag, 0.0)
        out[b:b + 1, :] = jnp.sum(power.T, axis=0, keepdims=True) * (
            1.0 / (mics * chunks * chunk_segs * T))

    def drain(c, carry):
        for index, (t2, m2) in enumerate(peers):
            push(c, index, t2, m2).wait_send()
        if Y == 2:
            for k in range(1, Z):
                forward(c, k).wait_send()
        return carry

    lax.fori_loop(0, chunks, drain, 0)


def per_device(T, M, samples, bin_ids, delays):
    segs, mics_here, length = samples.shape
    points, mics = delays.shape
    bin_count = bin_ids.shape[0]
    Y = 2 if M % 2 == 0 else 1
    Z = M // Y
    nb = bin_count // T
    chunk_segs = max(1, 16 // (2 * nb))
    chunks = segs // chunk_segs
    group = min(mics_here, 256)
    parts = mics_here // group
    slots = 4
    rows = chunk_segs * 2 * nb
    peers = T * Z - 1 + (T if Y == 2 else 0)
    dims = (T, Z, Y, bin_count, nb, chunk_segs, chunks, parts, group, slots)
    DMA = pltpu.SemaphoreType.DMA
    return pl.pallas_call(
        functools.partial(kernel, dims),
        out_shape=jax.ShapeDtypeStruct((nb, points), jnp.float32),
        in_specs=[
            pl.BlockSpec(memory_space=pltpu.SMEM),
            pl.BlockSpec(memory_space=pl.ANY),
            pl.BlockSpec(memory_space=pl.ANY),
        ],
        out_specs=pl.BlockSpec(memory_space=pltpu.VMEM),
        scratch_shapes=[
            pltpu.VMEM((2 * bin_count, length), jnp.bfloat16),
            pltpu.VMEM((slots, chunk_segs, group, length), jnp.bfloat16),
            pltpu.VMEM((points, mics), jnp.int32),
            pltpu.VMEM((chunks, T * rows, mics_here), jnp.bfloat16),
            pltpu.VMEM((M, chunks * T * rows, mics_here), jnp.bfloat16),
            pltpu.VMEM((nb, 2, points, mics), jnp.bfloat16),
            pltpu.VMEM((nb * 2 * points, chunks * T * rows), jnp.float32),
            DMA((slots,)),
            DMA(()),
            DMA((chunks, peers)),
            DMA((chunks, max(Z - 1, 1))),
            DMA((chunks, M)),
        ],
        compiler_params=pltpu.CompilerParams(
            collective_id=0, has_side_effects=True, vmem_limit_bytes=56 * 1024 * 1024),
        cost_estimate=pl.CostEstimate(
            flops=2 * samples.size * 2 * bin_count, bytes_accessed=samples.size * 2, transcendentals=0),
    )(bin_ids, samples, delays)


def solution(mesh):
    placed = (P("tm", "mic", None), P(), P("mic", None))
    return jax.shard_map(
        functools.partial(per_device, mesh.shape["tm"], mesh.shape["mic"]),
        mesh=mesh, in_specs=placed, out_specs=P("tm", "mic"), check_vma=False)
```

time: 143 us -> 49.7 us (0.35)
  the two profiles are of different devices: /device:TPU:0 before, /device:TPU:9 now
where the time goes in v1:
time: 49.7 us; the launch traced here: 49.5 us
  Pallas kernels  48.2 us (97%)
  local copies, waits for them, and re-layouts  1.26 us (3%)
    pallas_call x1, Pallas kernels, per_device(): pl.pallas_call(functools.partial(kernel, dims), out_shape=jax.ShapeDtypeS...  48.2 us
    unnamed x1, local copies, waits for them, and re-layouts  1.26 us

profile of v1, /device:TPU:9, one launch (start us, length us, event | category | flops | bytes accessed | tf_op | source)
XLA Modules:
  0.0 49.5 jit_solution(13847706413490481142)
XLA Ops:
  0.0 48.2 %shard_map.37 = f32[4,128]{1,0:T(4,128)} custom-call(s32[16]{0:T(128)} %bins.1, bf16[8,512,4096]{2,1,0:T(8,128)(2,1)} %samples.1, s32[128,4096]{1,0:T(8,128)} %delays.1), custom_call_target="tpu_custom_call" | custom-call | flops 1073741824 | bytes 33554432 | tf_op jit(solution)/shard_map/pallas_call | solution.py:256
  48.3 1.3 %copy.5 = f32[4,128]{1,0:T(4,128)} copy(f32[4,128]{1,0:T(4,128)} %shard_map.37) | data formatting | bytes 4096

commit v2 on v1

--- a/solution.py
+++ b/solution.py
@@ -108,7 +108,6 @@
 
     lax.fori_loop(0, length // 128, table_step, 0, unroll=4)
 
-    pltpu.make_async_copy(delays, delay, delay_sem).wait()
     own_scale = [bins[t * nb + b].astype(jnp.float32) * (1.0 / length) for b in range(nb)]
     point_part = points // steps
     width = 512 if mics % 512 == 0 else 128
@@ -155,6 +154,35 @@
         fetch(i, slot).wait()
         block = held[slot].reshape(chunk_segs * group, length)
         found = lax.dot_general(block, table[...], NT, preferred_element_type=jnp.float32)
+        found = [found[s * group:(s + 1) * group].T for s in range(chunk_segs)]
+        for t2 in range(T):
+            lines = [f[t2 * 2 * nb:(t2 + 1) * 2 * nb] for f in found]
+            spec[c, t2 * rows:(t2 + 1) * rows, pl.ds(pl.multiple_of(q * group, group), group)] = (
+                jnp.concatenate(lines, axis=0).astype(jnp.bfloat16))
+
+        @pl.when(i + slots < steps)
+        def _():
+            fetch(i + slots, slot).start()
+
+        @pl.when(q == parts - 1)
+        def _():
+            send_chunk(c)
+
+            @pl.when(c >= 2)
+            def _():
+                @pl.when(c < chunks - 1)
+                def _():
+                    pass_on(c - 2)
+
+        return carry
+
+    lax.fori_loop(0, steps, step, 0)
+
+    pltpu.make_async_copy(delays, delay, delay_sem).wait()
+    late = list(range(max(0, chunks - 3), chunks))
+    turn_of = {(n * steps) // len(late) + 1: c for n, c in enumerate(late[:-1])}
+
+    def steer_step(i, carry):
         first = pl.multiple_of(i * point_part, point_part)
         for start in range(0, mics, width):
             turns = delay[pl.ds(first, point_part), start:start + width].astype(jnp.float32)
@@ -162,28 +190,15 @@
                 cosine, sine = cos_sin_turns(turns * own_scale[b])
                 steer[b, 0, pl.ds(first, point_part), start:start + width] = cosine.astype(jnp.bfloat16)
                 steer[b, 1, pl.ds(first, point_part), start:start + width] = sine.astype(jnp.bfloat16)
-        found = [found[s * group:(s + 1) * group].T for s in range(chunk_segs)]
-        for t2 in range(T):
-            lines = [f[t2 * 2 * nb:(t2 + 1) * 2 * nb] for f in found]
-            spec[c, t2 * rows:(t2 + 1) * rows, pl.ds(pl.multiple_of(q * group, group), group)] = (
-                jnp.concatenate(lines, axis=0).astype(jnp.bfloat16))
-
-        @pl.when(i + slots < steps)
-        def _():
-            fetch(i + slots, slot).start()
-
-        @pl.when(q == parts - 1)
-        def _():
-            send_chunk(c)
-
-            @pl.when(c >= 1)
+        for turn, c in turn_of.items():
+            @pl.when(i == turn)
             def _():
-                pass_on(c - 1)
-
-        return carry
-
-    lax.fori_loop(0, steps, step, 0)
-    pass_on(chunks - 1)
+                pass_on(c)
+
+        return carry
+
+    lax.fori_loop(0, steps, steer_step, 0)
+    pass_on(late[-1])
 
     acc[...] = jnp.zeros_like(acc)
 

time: 49.7 us -> 45.4 us (0.913)
  the two profiles are of different devices: /device:TPU:9 before, /device:TPU:0 now
where the time goes in v2:
time: 45.4 us; the launch traced here: 44.9 us
  Pallas kernels  43.6 us (96%)
  local copies, waits for them, and re-layouts  1.26 us (3%)
    pallas_call x1, Pallas kernels, per_device(): pl.pallas_call(functools.partial(kernel, dims), out_shape=jax.ShapeDtypeS...  43.6 us
    unnamed x1, local copies, waits for them, and re-layouts  1.26 us

profile of v2, /device:TPU:0, one launch (start us, length us, event | category | flops | bytes accessed | tf_op | source)
XLA Modules:
  0.0 44.9 jit_solution(2693455689234674623)
XLA Ops:
  0.0 43.6 %shard_map.37 = f32[4,128]{1,0:T(4,128)} custom-call(s32[16]{0:T(128)} %bins.1, bf16[8,512,4096]{2,1,0:T(8,128)(2,1)} %samples.1, s32[128,4096]{1,0:T(8,128)} %delays.1), custom_call_target="tpu_custom_call" | custom-call | flops 1073741824 | bytes 33554432 | tf_op jit(solution)/shard_map/pallas_call | solution.py:271
  43.6 1.3 %copy.5 = f32[4,128]{1,0:T(4,128)} copy(f32[4,128]{1,0:T(4,128)} %shard_map.37) | data formatting | bytes 4096

commit v3 on v1

v3 whole, which is shorter than its diff:
```python
import functools
import math

import jax
import jax.numpy as jnp
import numpy as np
from jax import lax
from jax.experimental import pallas as pl
from jax.experimental.pallas import tpu as pltpu
from jax.sharding import PartitionSpec as P

MESH = pl.DeviceIdType.MESH
NT = (((1,), (1,)), ((), ()))


def fit(function, count):
    nodes = 0.125 + 0.125 * np.cos(np.pi * (np.arange(64) + 0.5) / 64)
    series = np.polynomial.chebyshev.Chebyshev.fit(nodes, function(np.sqrt(nodes)), count - 1, domain=[0, 0.25])
    return [float(c) for c in series.convert(kind=np.polynomial.Polynomial).coef]


SIN_HALF = fit(lambda r: np.sin(np.pi * r) / r, 5)
COS_HALF = fit(lambda r: np.cos(np.pi * r), 6)


def horner(coefficients, y):
    total = coefficients[-1]
    for c in coefficients[-2::-1]:
        total = total * y + c
    return total


def fraction(turns):
    return turns - ((turns + 12582912.0) - 12582912.0)


def cos_turns(turns):
    r = fraction(turns)
    s = r * horner(SIN_HALF, r * r)
    return 1.0 - (s + s) * s


def cos_sin_turns(turns):
    r = fraction(turns)
    y = r * r
    s = r * horner(SIN_HALF, y)
    twice = s + s
    return 1.0 - twice * s, twice * horner(COS_HALF, y)


def kernel(dims, bins, samples, delays, out, table, held, delay, quarter, other_delay, spec, gath, steer, acc,
           power_out, power_in, sample_sem, delay_sem, send_sem, fwd_sem, recv_sem, quarter_send, quarter_recv,
           power_sem):
    T, Z, Y, bin_count, nb, wb, rows, chunk_segs, parts, group, steps, slots = dims
    mics_here, length = samples.shape[1], samples.shape[2]
    points, mics = delays.shape
    seg_groups = steps // parts
    t, m = lax.axis_index("tm"), lax.axis_index("mic")
    z, y = lax.div(m, Y), lax.rem(m, Y)
    side = lax.rem(z, 2)

    def mic_of(z2, y2):
        return z2 * Y + y2

    def fetch(i, slot):
        c, q = lax.div(i, parts), lax.rem(i, parts)
        return pltpu.make_async_copy(
            samples.at[pl.ds(c * chunk_segs, chunk_segs), pl.ds(pl.multiple_of(q * group, group), group)],
            held.at[slot], sample_sem.at[slot])

    pltpu.make_async_copy(delays, delay, delay_sem).start()
    for i in range(min(slots, steps)):
        fetch(i, i).start()

    near = [(lax.rem(t + a, T), lax.rem(z + k, Z), y) for k in range(Z) for a in range(T) if k or a]
    across = [(lax.rem(t + a, T), z, 1 - y) for a in range(T)]
    peers = near + across
    partner = mic_of(z + 1 - 2 * side, y)
    barrier = pltpu.get_barrier_semaphore()
    for t2, z2, y2 in peers:
        pl.semaphore_signal(barrier, inc=1, device_id={"tm": t2, "mic": mic_of(z2, y2)}, device_id_type=MESH)

    table_rows = 2 * bin_count
    row = lax.broadcasted_iota(jnp.int32, (table_rows, 128), 0)
    lane = lax.broadcasted_iota(jnp.int32, (table_rows, 128), 1)
    bin_of = (row // (2 * wb)) * wb + row % wb
    scale = jnp.zeros((table_rows, 128), jnp.float32)
    for i in range(bin_count):
        scale = jnp.where(bin_of == i, bins[i].astype(jnp.float32) * (1.0 / length), scale)
    shift = jnp.where((row // wb) % 2 == 1, jnp.float32(0.25), jnp.float32(0.0))
    lane8 = lax.broadcasted_iota(jnp.int32, (8, 128), 1)

    def window_at(j, like):
        return 0.5 - 0.5 * cos_turns((like + j * 128).astype(jnp.float32) * (1.0 / length))

    def norm_step(j, total):
        w = window_at(j, lane8)
        return total + w * w

    norm = jnp.sum(lax.fori_loop(0, length // 128, norm_step, jnp.zeros((8, 128), jnp.float32), unroll=4),
                   axis=1, keepdims=True)[0:1]
    inverse = 1.0 / jnp.sqrt(norm)

    def table_step(j, carry):
        w = window_at(j, lane8)[0:1] * inverse
        turns = (lane + j * 128).astype(jnp.float32) * scale + shift
        table[:, pl.ds(pl.multiple_of(j * 128, 128), 128)] = (w * cos_turns(turns)).astype(jnp.bfloat16)
        return carry

    lax.fori_loop(0, length // 128, table_step, 0, unroll=4)

    own_scale = [bins[t * nb + side * wb + b].astype(jnp.float32) * (1.0 / length) for b in range(wb)]
    width = 512 if mics % 512 == 0 else 128
    share = points // T

    def block_of(i, m2):
        g, q = lax.div(i, parts), lax.rem(i, parts)
        return gath.at[m2, pl.ds(pl.multiple_of(g * T * rows, T * rows), T * rows),
                       pl.ds(pl.multiple_of(q * group, group), group)]

    def slot_of(i):
        g, q = lax.div(i, parts), lax.rem(i, parts)
        return gath.at[m, pl.ds(pl.multiple_of(g * T * rows + t * rows, rows), rows),
                       pl.ds(pl.multiple_of(q * group, group), group)]

    def source_of(i, t2, z2):
        worker = t2 * 2 + lax.rem(z2, 2)
        return spec.at[i, pl.ds(pl.multiple_of(worker * rows, rows), rows)]

    def push(i, index, t2, z2, y2):
        return pltpu.make_async_remote_copy(
            src_ref=source_of(i, t2, z2), dst_ref=slot_of(i),
            send_sem=send_sem.at[i, index], recv_sem=recv_sem.at[i, m],
            device_id={"tm": t2, "mic": mic_of(z2, y2)}, device_id_type=MESH)

    def forward(i, k):
        m2 = mic_of(lax.rem(z + k, Z), y)
        return pltpu.make_async_remote_copy(
            src_ref=block_of(i, m2), dst_ref=block_of(i, m2),
            send_sem=fwd_sem.at[i, k - 1], recv_sem=recv_sem.at[i, m2],
            device_id={"tm": t, "mic": mic_of(z, 1 - y)}, device_id_type=MESH)

    def arrived(i, m2):
        pltpu.make_async_copy(block_of(i, m2), block_of(i, m2), recv_sem.at[i, m2]).wait()

    def send_chunk(i):
        for index, peer in enumerate(peers):
            push(i, index, *peer).start()
        pltpu.make_async_copy(source_of(i, t, z), slot_of(i), recv_sem.at[i, m]).start()

    def pass_on(i):
        for k in range(1, Z):
            arrived(i, mic_of(lax.rem(z + k, Z), y))
            forward(i, k).start()

    def share_of(t2):
        return other_delay.at[pl.ds(pl.multiple_of(t2 * share, share), share)]

    def give_share():
        return pltpu.make_async_remote_copy(
            src_ref=quarter, dst_ref=share_of(t), send_sem=quarter_send.at[0], recv_sem=quarter_recv.at[t],
            device_id={"tm": t, "mic": partner}, device_id_type=MESH)

    def share_on(a):
        return pltpu.make_async_remote_copy(
            src_ref=share_of(t), dst_ref=share_of(t), send_sem=quarter_send.at[a], recv_sem=quarter_recv.at[t],
            device_id={"tm": lax.rem(t + a, T), "mic": m}, device_id_type=MESH)

    def share_arrived(t2):
        pltpu.make_async_copy(share_of(t2), share_of(t2), quarter_recv.at[t2]).wait()

    pltpu.make_async_copy(delays, delay, delay_sem).wait()
    quarter[...] = delay[pl.ds(pl.multiple_of(t * share, share), share), :].astype(jnp.int16)
    pl.semaphore_wait(barrier, len(peers))
    give_share().start()

    def step(i, carry):
        slot = lax.rem(i, slots)
        fetch(i, slot).wait()
        block = held[slot].reshape(chunk_segs * group, length)
        found = lax.dot_general(block, table[...], NT, preferred_element_type=jnp.float32)
        found = [found[s * group:(s + 1) * group].T for s in range(chunk_segs)]
        for worker in range(2 * T):
            lines = [f[worker * 2 * wb:(worker + 1) * 2 * wb] for f in found]
            spec[i, worker * rows:(worker + 1) * rows, :] = jnp.concatenate(lines, axis=0).astype(jnp.bfloat16)

        @pl.when(i + slots < steps)
        def _():
            fetch(i + slots, slot).start()

        send_chunk(i)

        @pl.when(i == 1)
        def _():
            share_arrived(t)
            for a in range(1, T):
                share_on(a).start()

        @pl.when(i >= 2)
        def _():
            pass_on(i - 2)

        return carry

    lax.fori_loop(0, steps, step, 0)

    piece = 16
    pieces = points // piece
    turn_of = {pieces // 8: steps - 2, pieces // 2: steps - 1}

    def steer_step(half, i):
        first = pl.multiple_of(i * piece, piece)
        source = other_delay if half else delay
        for start in range(0, mics, width):
            turns = source[pl.ds(first, piece), start:start + width].astype(jnp.int32).astype(jnp.float32)
            for b in range(wb):
                cosine, sine = cos_sin_turns(turns * own_scale[b])
                steer[b, 0, half, pl.ds(first, piece), start:start + width] = cosine.astype(jnp.bfloat16)
                steer[b, 1, half, pl.ds(first, piece), start:start + width] = sine.astype(jnp.bfloat16)

    def own_step(i, carry):
        steer_step(0, i)
        for turn, late in turn_of.items():
            @pl.when(i == turn)
            def _():
                pass_on(late)

        return carry

    def partner_step(i, carry):
        steer_step(1, i)
        return carry

    lax.fori_loop(0, pieces, own_step, 0)
    for a in range(1, T):
        share_arrived(lax.rem(t + a, T))
    lax.fori_loop(0, pieces, partner_step, 0)

    acc[...] = jnp.zeros_like(acc)

    def add_block(m2):
        columns = pl.ds(pl.multiple_of(m2 * mics_here, mics_here), mics_here)
        lhs = steer[:, :, :, :, columns].reshape(wb * 4 * points, mics_here)
        acc[...] += lax.dot_general(lhs, gath[m2], NT, preferred_element_type=jnp.float32)

    def own_y(k, carry):
        m2 = mic_of(lax.rem(z + k, Z), y)

        @pl.when(k == 0)
        def _():
            for i in range(steps):
                arrived(i, m2)

        add_block(m2)
        return carry

    lax.fori_loop(0, Z, own_y, 0)

    def other_y(k, carry):
        m2 = mic_of(lax.rem(z + k, Z), 1 - y)
        for i in range(steps):
            arrived(i, m2)
        add_block(m2)
        return carry

    lax.fori_loop(0, Z, other_y, 0)

    columns = seg_groups * T * rows
    column = lax.broadcasted_iota(jnp.int32, (2 * points, columns), 1)
    own, theirs = [], []
    for b in range(wb):
        along_cos = acc[(4 * b) * points:(4 * b + 2) * points]
        along_sin = acc[(4 * b + 2) * points:(4 * b + 4) * points]
        real = along_cos - pltpu.roll(along_sin, columns - wb, axis=1)
        imag = pltpu.roll(along_cos, columns - wb, axis=1) + along_sin
        power = jnp.where(column % (2 * wb) == b, real * real + imag * imag, 0.0)
        total = jnp.sum(power.T, axis=0, keepdims=True) * (1.0 / (mics * seg_groups * chunk_segs * T))
        own.append(total[:, :points])
        theirs.append(total[:, points:])
    power_out[...] = jnp.zeros_like(power_out)
    power_out[0:wb, :] = jnp.concatenate(theirs, axis=0)
    swap = pltpu.make_async_remote_copy(
        src_ref=power_out, dst_ref=power_in, send_sem=power_sem.at[0], recv_sem=power_sem.at[1],
        device_id={"tm": t, "mic": partner}, device_id_type=MESH)
    swap.start()

    def drain(i, carry):
        for index, peer in enumerate(peers):
            push(i, index, *peer).wait_send()
        for k in range(1, Z):
            forward(i, k).wait_send()
        return carry

    lax.fori_loop(0, steps, drain, 0)
    give_share().wait_send()
    for a in range(1, T):
        share_on(a).wait_send()
    swap.wait()
    own = jnp.concatenate(own, axis=0)
    came = power_in[0:wb, :]
    out[0:wb, :] = jnp.where(side == 0, own, came)
    out[wb:2 * wb, :] = jnp.where(side == 0, came, own)


def per_device(T, M, samples, bin_ids, delays):
    segs, mics_here, length = samples.shape
    points, mics = delays.shape
    bin_count = bin_ids.shape[0]
    Y = 2
    Z = M // Y
    nb = bin_count // T
    wb = nb // 2
    chunk_segs = max(1, 16 // (2 * wb))
    rows = chunk_segs * 2 * wb
    group = min(mics_here, 256)
    parts = mics_here // group
    steps = segs // chunk_segs * parts
    slots = min(steps, 3)
    columns = segs // chunk_segs * T * rows
    peers = T * Z - 1 + T
    dims = (T, Z, Y, bin_count, nb, wb, rows, chunk_segs, parts, group, steps, slots)
    DMA = pltpu.SemaphoreType.DMA
    return pl.pallas_call(
        functools.partial(kernel, dims),
        out_shape=jax.ShapeDtypeStruct((nb, points), jnp.float32),
        in_specs=[
            pl.BlockSpec(memory_space=pltpu.SMEM),
            pl.BlockSpec(memory_space=pl.ANY),
            pl.BlockSpec(memory_space=pl.ANY),
        ],
        out_specs=pl.BlockSpec(memory_space=pltpu.VMEM),
        scratch_shapes=[
            pltpu.VMEM((2 * bin_count, length), jnp.bfloat16),
            pltpu.VMEM((slots, chunk_segs, group, length), jnp.bfloat16),
            pltpu.VMEM((points, mics), jnp.int32),
            pltpu.VMEM((points // T, mics), jnp.int16),
            pltpu.VMEM((points, mics), jnp.int16),
            pltpu.VMEM((steps, 2 * T * rows, group), jnp.bfloat16),
            pltpu.VMEM((M, columns, mics_here), jnp.bfloat16),
            pltpu.VMEM((wb, 2, 2, points, mics), jnp.bfloat16),
            pltpu.VMEM((wb * 4 * points, columns), jnp.float32),
            pltpu.VMEM((8, points), jnp.float32),
            pltpu.VMEM((8, points), jnp.float32),
            DMA((slots,)),
            DMA(()),
            DMA((steps, peers)),
            DMA((steps, Z - 1)),
            DMA((steps, M)),
            DMA((T,)),
            DMA((T,)),
            DMA((2,)),
        ],
        compiler_params=pltpu.CompilerParams(
            collective_id=0, has_side_effects=True, vmem_limit_bytes=56 * 1024 * 1024),
        cost_estimate=pl.CostEstimate(
            flops=2 * samples.size * 2 * bin_count, bytes_accessed=samples.size * 2, transcendentals=0),
    )(bin_ids, samples, delays)


def solution(mesh):
    placed = (P("tm", "mic", None), P(), P("mic", None))
    return jax.shard_map(
        functools.partial(per_device, mesh.shape["tm"], mesh.shape["mic"]),
        mesh=mesh, in_specs=placed, out_specs=P("tm", "mic"), check_vma=False)
```

time: 49.7 us -> 45.6 us (0.918)
  the two profiles are of different devices: /device:TPU:9 before, /device:TPU:0 now
where the time goes in v3:
time: 45.6 us; the launch traced here: 45 us
  Pallas kernels  43.8 us (96%)
  local copies, waits for them, and re-layouts  1.26 us (3%)
    pallas_call x1, Pallas kernels, per_device(): pl.pallas_call(functools.partial(kernel, dims), out_shape=jax.ShapeDtypeS...  43.8 us
    unnamed x1, local copies, waits for them, and re-layouts  1.26 us

profile of v3, /device:TPU:0, one launch (start us, length us, event | category | flops | bytes accessed | tf_op | source)
XLA Modules:
  0.0 45.0 jit_solution(17252683845487204178)
XLA Ops:
  0.0 43.8 %shard_map.37 = f32[4,128]{1,0:T(4,128)} custom-call(s32[16]{0:T(128)} %bins.1, bf16[8,512,4096]{2,1,0:T(8,128)(2,1)} %samples.1, s32[128,4096]{1,0:T(8,128)} %delays.1), custom_call_target="tpu_custom_call" | custom-call | flops 1073741824 | bytes 33554432 | tf_op jit(solution)/shard_map/pallas_call | solution.py:323
  43.8 1.3 %copy.5 = f32[4,128]{1,0:T(4,128)} copy(f32[4,128]{1,0:T(4,128)} %shard_map.37) | data formatting | bytes 4096

commit v4 on v3

--- a/solution.py
+++ b/solution.py
@@ -19,8 +19,8 @@
     return [float(c) for c in series.convert(kind=np.polynomial.Polynomial).coef]
 
 
-SIN_HALF = fit(lambda r: np.sin(np.pi * r) / r, 5)
-COS_HALF = fit(lambda r: np.cos(np.pi * r), 6)
+SIN_HALF = fit(lambda r: math.sqrt(2) * np.sin(np.pi * r) / r, 5)
+COS_HALF = fit(lambda r: math.sqrt(2) * np.cos(np.pi * r), 5)
 
 
 def horner(coefficients, y):
@@ -37,15 +37,14 @@
 def cos_turns(turns):
     r = fraction(turns)
     s = r * horner(SIN_HALF, r * r)
-    return 1.0 - (s + s) * s
+    return 1.0 - s * s
 
 
 def cos_sin_turns(turns):
     r = fraction(turns)
     y = r * r
     s = r * horner(SIN_HALF, y)
-    twice = s + s
-    return 1.0 - twice * s, twice * horner(COS_HALF, y)
+    return 1.0 - s * s, s * horner(COS_HALF, y)
 
 
 def kernel(dims, bins, samples, delays, out, table, held, delay, quarter, other_delay, spec, gath, steer, acc,
@@ -174,12 +173,35 @@
     pl.semaphore_wait(barrier, len(peers))
     give_share().start()
 
+    def trig(half, first, count, start):
+        source = other_delay if half else delay
+        turns = source[pl.ds(first, count), start:start + width].astype(jnp.int32).astype(jnp.float32)
+        for b in range(wb):
+            cosine, sine = cos_sin_turns(turns * own_scale[b])
+            steer[half, b, 0, pl.ds(first, count), start:start + width] = cosine.astype(jnp.bfloat16)
+            steer[half, b, 1, pl.ds(first, count), start:start + width] = sine.astype(jnp.bfloat16)
+
+    piece = 16
+
+    def trig_pieces(half, first, count):
+        return [functools.partial(trig, half, pl.multiple_of(first + lead, piece), piece, start)
+                for lead in range(0, count, piece) for start in range(0, mics, width)]
+
+    at_once = 2 if chunk_segs % 2 == 0 else 1
+    slices = chunk_segs // at_once
+    points_step = points // steps
+
     def step(i, carry):
         slot = lax.rem(i, slots)
         fetch(i, slot).wait()
-        block = held[slot].reshape(chunk_segs * group, length)
-        found = lax.dot_general(block, table[...], NT, preferred_element_type=jnp.float32)
-        found = [found[s * group:(s + 1) * group].T for s in range(chunk_segs)]
+        todo = trig_pieces(0, pl.multiple_of(i * points_step, points_step), points_step)
+        found = []
+        for n in range(slices):
+            block = held[slot, n * at_once:(n + 1) * at_once].reshape(at_once * group, length)
+            part = lax.dot_general(block, table[...], NT, preferred_element_type=jnp.float32)
+            for work in todo[n * len(todo) // slices:(n + 1) * len(todo) // slices]:
+                work()
+            found += [part[s * group:(s + 1) * group].T for s in range(at_once)]
         for worker in range(2 * T):
             lines = [f[worker * 2 * wb:(worker + 1) * 2 * wb] for f in found]
             spec[i, worker * rows:(worker + 1) * rows, :] = jnp.concatenate(lines, axis=0).astype(jnp.bfloat16)
@@ -204,81 +226,72 @@
 
     lax.fori_loop(0, steps, step, 0)
 
-    piece = 16
-    pieces = points // piece
-    turn_of = {pieces // 8: steps - 2, pieces // 2: steps - 1}
-
-    def steer_step(half, i):
-        first = pl.multiple_of(i * piece, piece)
-        source = other_delay if half else delay
-        for start in range(0, mics, width):
-            turns = source[pl.ds(first, piece), start:start + width].astype(jnp.int32).astype(jnp.float32)
-            for b in range(wb):
-                cosine, sine = cos_sin_turns(turns * own_scale[b])
-                steer[b, 0, half, pl.ds(first, piece), start:start + width] = cosine.astype(jnp.bfloat16)
-                steer[b, 1, half, pl.ds(first, piece), start:start + width] = sine.astype(jnp.bfloat16)
-
-    def own_step(i, carry):
-        steer_step(0, i)
-        for turn, late in turn_of.items():
-            @pl.when(i == turn)
-            def _():
-                pass_on(late)
-
-        return carry
-
-    def partner_step(i, carry):
-        steer_step(1, i)
-        return carry
-
-    lax.fori_loop(0, pieces, own_step, 0)
+    acc[...] = jnp.zeros_like(acc)
     for a in range(1, T):
         share_arrived(lax.rem(t + a, T))
-    lax.fori_loop(0, pieces, partner_step, 0)
-
-    acc[...] = jnp.zeros_like(acc)
-
-    def add_block(m2):
+
+    def add_block(half, m2):
         columns = pl.ds(pl.multiple_of(m2 * mics_here, mics_here), mics_here)
-        lhs = steer[:, :, :, :, columns].reshape(wb * 4 * points, mics_here)
-        acc[...] += lax.dot_general(lhs, gath[m2], NT, preferred_element_type=jnp.float32)
-
-    def own_y(k, carry):
+        lhs = steer[half, :, :, :, columns].reshape(wb * 2 * points, mics_here)
+        acc[half] += lax.dot_general(lhs, gath[m2], NT, preferred_element_type=jnp.float32)
+
+    trig_blocks = points // piece
+    each = -(-trig_blocks // Z)
+
+    def own_points(k, carry):
         m2 = mic_of(lax.rem(z + k, Z), y)
 
         @pl.when(k == 0)
         def _():
+            pass_on(steps - 2)
             for i in range(steps):
                 arrived(i, m2)
 
-        add_block(m2)
-        return carry
-
-    lax.fori_loop(0, Z, own_y, 0)
+        @pl.when(k == 1)
+        def _():
+            pass_on(steps - 1)
+
+        add_block(0, m2)
+        for n in range(each):
+            block = jnp.minimum(k * each + n, trig_blocks - 1)
+            for work in trig_pieces(1, pl.multiple_of(block * piece, piece), piece):
+                work()
+        return carry
+
+    lax.fori_loop(0, Z, own_points, 0)
+
+    def partner_points(k, carry):
+        add_block(1, mic_of(lax.rem(z + k, Z), y))
+        return carry
+
+    lax.fori_loop(0, Z, partner_points, 0)
 
     def other_y(k, carry):
         m2 = mic_of(lax.rem(z + k, Z), 1 - y)
         for i in range(steps):
             arrived(i, m2)
-        add_block(m2)
+        add_block(0, m2)
+        add_block(1, m2)
         return carry
 
     lax.fori_loop(0, Z, other_y, 0)
 
     columns = seg_groups * T * rows
-    column = lax.broadcasted_iota(jnp.int32, (2 * points, columns), 1)
-    own, theirs = [], []
-    for b in range(wb):
-        along_cos = acc[(4 * b) * points:(4 * b + 2) * points]
-        along_sin = acc[(4 * b + 2) * points:(4 * b + 4) * points]
-        real = along_cos - pltpu.roll(along_sin, columns - wb, axis=1)
-        imag = pltpu.roll(along_cos, columns - wb, axis=1) + along_sin
-        power = jnp.where(column % (2 * wb) == b, real * real + imag * imag, 0.0)
-        total = jnp.sum(power.T, axis=0, keepdims=True) * (1.0 / (mics * seg_groups * chunk_segs * T))
-        own.append(total[:, :points])
-        theirs.append(total[:, points:])
+    column = lax.broadcasted_iota(jnp.int32, (points, columns), 1)
+    totals = []
+    for half in range(2):
+        lines = []
+        for b in range(wb):
+            along_cos = acc[half, (2 * b) * points:(2 * b + 1) * points]
+            along_sin = acc[half, (2 * b + 1) * points:(2 * b + 2) * points]
+            real = along_cos - pltpu.roll(along_sin, columns - wb, axis=1)
+            imag = pltpu.roll(along_cos, columns - wb, axis=1) + along_sin
+            power = jnp.where(column % (2 * wb) == b, real * real + imag * imag, 0.0)
+            lines.append(jnp.sum(power.T, axis=0, keepdims=True))
+        totals.append(jnp.concatenate(lines, axis=0) * (1.0 / (mics * seg_groups * chunk_segs * T)))
+    own, theirs = totals
     power_out[...] = jnp.zeros_like(power_out)
-    power_out[0:wb, :] = jnp.concatenate(theirs, axis=0)
+    power_out[0:wb, :] = theirs
     swap = pltpu.make_async_remote_copy(
         src_ref=power_out, dst_ref=power_in, send_sem=power_sem.at[0], recv_sem=power_sem.at[1],
         device_id={"tm": t, "mic": partner}, device_id_type=MESH)
@@ -296,7 +309,6 @@
     for a in range(1, T):
         share_on(a).wait_send()
     swap.wait()
-    own = jnp.concatenate(own, axis=0)
     came = power_in[0:wb, :]
     out[0:wb, :] = jnp.where(side == 0, own, came)
     out[wb:2 * wb, :] = jnp.where(side == 0, came, own)
@@ -337,8 +349,8 @@
             pltpu.VMEM((points, mics), jnp.int16),
             pltpu.VMEM((steps, 2 * T * rows, group), jnp.bfloat16),
             pltpu.VMEM((M, columns, mics_here), jnp.bfloat16),
-            pltpu.VMEM((wb, 2, 2, points, mics), jnp.bfloat16),
-            pltpu.VMEM((wb * 4 * points, columns), jnp.float32),
+            pltpu.VMEM((2, wb, 2, points, mics), jnp.bfloat16),
+            pltpu.VMEM((2, wb * 2 * points, columns), jnp.float32),
             pltpu.VMEM((8, points), jnp.float32),
             pltpu.VMEM((8, points), jnp.float32),
             DMA((slots,)),

time: 45.6 us -> 48.3 us (1.059)
  Pallas kernels: 43.8 us -> 46.9 us
    pallas_call x1, Pallas kernels: 43.8 us -> 46.9 us  [per_device(): pl.pallas_call(functools.partial(kernel, dims), out_shape=jax.ShapeDtypeS...]
where the time goes in v4:
time: 48.3 us; the launch traced here: 48.2 us
  Pallas kernels  46.9 us (97%)
  local copies, waits for them, and re-layouts  1.26 us (3%)
    pallas_call x1, Pallas kernels, per_device(): pl.pallas_call(functools.partial(kernel, dims), out_shape=jax.ShapeDtypeS...  46.9 us
    unnamed x1, local copies, waits for them, and re-layouts  1.26 us

profile of v4, /device:TPU:0, one launch (start us, length us, event | category | flops | bytes accessed | tf_op | source)
XLA Modules:
  0.0 48.2 jit_solution(9618530213936940489)
XLA Ops:
  0.0 46.9 %shard_map.37 = f32[4,128]{1,0:T(4,128)} custom-call(s32[16]{0:T(128)} %bins.1, bf16[8,512,4096]{2,1,0:T(8,128)(2,1)} %samples.1, s32[128,4096]{1,0:T(8,128)} %delays.1), custom_call_target="tpu_custom_call" | custom-call | flops 1073741824 | bytes 33554432 | tf_op jit(solution)/shard_map/pallas_call | solution.py:335
  46.9 1.3 %copy.5 = f32[4,128]{1,0:T(4,128)} copy(f32[4,128]{1,0:T(4,128)} %shard_map.37) | data formatting | bytes 4096

commit v5 on v4

--- a/solution.py
+++ b/solution.py
@@ -112,15 +112,11 @@
     width = 512 if mics % 512 == 0 else 128
     share = points // T
 
-    def block_of(i, m2):
-        g, q = lax.div(i, parts), lax.rem(i, parts)
-        return gath.at[m2, pl.ds(pl.multiple_of(g * T * rows, T * rows), T * rows),
-                       pl.ds(pl.multiple_of(q * group, group), group)]
-
-    def slot_of(i):
-        g, q = lax.div(i, parts), lax.rem(i, parts)
-        return gath.at[m, pl.ds(pl.multiple_of(g * T * rows + t * rows, rows), rows),
-                       pl.ds(pl.multiple_of(q * group, group), group)]
+    def block_of(g, m2):
+        return gath.at[m2, pl.ds(pl.multiple_of(g * T * rows, T * rows), T * rows)]
+
+    def slot_of(g):
+        return gath.at[m, pl.ds(pl.multiple_of(g * T * rows + t * rows, rows), rows)]
 
     def source_of(i, t2, z2):
         worker = t2 * 2 + lax.rem(z2, 2)
@@ -187,30 +183,25 @@
         return [functools.partial(trig, half, pl.multiple_of(first + lead, piece), piece, start)
                 for lead in range(0, count, piece) for start in range(0, mics, width)]
 
-    at_once = 2 if chunk_segs % 2 == 0 else 1
-    slices = chunk_segs // at_once
-    points_step = points // steps
-
     def step(i, carry):
         slot = lax.rem(i, slots)
+        g, q = lax.div(i, parts), lax.rem(i, parts)
         fetch(i, slot).wait()
-        todo = trig_pieces(0, pl.multiple_of(i * points_step, points_step), points_step)
-        found = []
-        for n in range(slices):
-            block = held[slot, n * at_once:(n + 1) * at_once].reshape(at_once * group, length)
-            part = lax.dot_general(block, table[...], NT, preferred_element_type=jnp.float32)
-            for work in todo[n * len(todo) // slices:(n + 1) * len(todo) // slices]:
-                work()
-            found += [part[s * group:(s + 1) * group].T for s in range(at_once)]
+        block = held[slot].reshape(chunk_segs * group, length)
+        found = lax.dot_general(block, table[...], NT, preferred_element_type=jnp.float32)
+        found = [found[s * group:(s + 1) * group].T for s in range(chunk_segs)]
         for worker in range(2 * T):
             lines = [f[worker * 2 * wb:(worker + 1) * 2 * wb] for f in found]
-            spec[i, worker * rows:(worker + 1) * rows, :] = jnp.concatenate(lines, axis=0).astype(jnp.bfloat16)
+            spec[g, worker * rows:(worker + 1) * rows, pl.ds(pl.multiple_of(q * group, group), group)] = (
+                jnp.concatenate(lines, axis=0).astype(jnp.bfloat16))
 
         @pl.when(i + slots < steps)
         def _():
             fetch(i + slots, slot).start()
 
-        send_chunk(i)
+        @pl.when(q == parts - 1)
+        def _():
+            send_chunk(g)
 
         @pl.when(i == 1)
         def _():
@@ -218,47 +209,50 @@
             for a in range(1, T):
                 share_on(a).start()
 
-        @pl.when(i >= 2)
-        def _():
-            pass_on(i - 2)
-
         return carry
 
     lax.fori_loop(0, steps, step, 0)
 
     acc[...] = jnp.zeros_like(acc)
-    for a in range(1, T):
-        share_arrived(lax.rem(t + a, T))
 
     def add_block(half, m2):
         columns = pl.ds(pl.multiple_of(m2 * mics_here, mics_here), mics_here)
         lhs = steer[half, :, :, :, columns].reshape(wb * 2 * points, mics_here)
         acc[half] += lax.dot_general(lhs, gath[m2], NT, preferred_element_type=jnp.float32)
 
-    trig_blocks = points // piece
-    each = -(-trig_blocks // Z)
+    def own_trig(i, carry):
+        for work in trig_pieces(0, pl.multiple_of(i * piece, piece), piece):
+            work()
+
+        @pl.when(i == 0)
+        def _():
+            for g in range(seg_groups - 1):
+                pass_on(g)
+
+        return carry
+
+    def partner_trig(i, carry):
+        for work in trig_pieces(1, pl.multiple_of(i * piece, piece), piece):
+            work()
+        return carry
 
     def own_points(k, carry):
         m2 = mic_of(lax.rem(z + k, Z), y)
 
         @pl.when(k == 0)
         def _():
-            pass_on(steps - 2)
-            for i in range(steps):
-                arrived(i, m2)
-
-        @pl.when(k == 1)
-        def _():
-            pass_on(steps - 1)
+            pass_on(seg_groups - 1)
+            for g in range(seg_groups):
+                arrived(g, m2)
 
         add_block(0, m2)
-        for n in range(each):
-            block = jnp.minimum(k * each + n, trig_blocks - 1)
-            for work in trig_pieces(1, pl.multiple_of(block * piece, piece), piece):
-                work()
-        return carry
-
+        return carry
+
+    lax.fori_loop(0, points // piece, own_trig, 0)
     lax.fori_loop(0, Z, own_points, 0)
+    for a in range(1, T):
+        share_arrived(lax.rem(t + a, T))
+    lax.fori_loop(0, points // piece, partner_trig, 0)
 
     def partner_points(k, carry):
         add_block(1, mic_of(lax.rem(z + k, Z), y))
@@ -268,8 +262,8 @@
 
     def other_y(k, carry):
         m2 = mic_of(lax.rem(z + k, Z), 1 - y)
-        for i in range(steps):
-            arrived(i, m2)
+        for g in range(seg_groups):
+            arrived(g, m2)
         add_block(0, m2)
         add_block(1, m2)
         return carry
@@ -304,7 +298,7 @@
             forward(i, k).wait_send()
         return carry
 
-    lax.fori_loop(0, steps, drain, 0)
+    lax.fori_loop(0, seg_groups, drain, 0)
     give_share().wait_send()
     for a in range(1, T):
         share_on(a).wait_send()
@@ -326,9 +320,10 @@
     rows = chunk_segs * 2 * wb
     group = min(mics_here, 256)
     parts = mics_here // group
-    steps = segs // chunk_segs * parts
+    groups = segs // chunk_segs
+    steps = groups * parts
     slots = min(steps, 3)
-    columns = segs // chunk_segs * T * rows
+    columns = groups * T * rows
     peers = T * Z - 1 + T
     dims = (T, Z, Y, bin_count, nb, wb, rows, chunk_segs, parts, group, steps, slots)
     DMA = pltpu.SemaphoreType.DMA
@@ -347,7 +342,7 @@
             pltpu.VMEM((points, mics), jnp.int32),
             pltpu.VMEM((points // T, mics), jnp.int16),
             pltpu.VMEM((points, mics), jnp.int16),
-            pltpu.VMEM((steps, 2 * T * rows, group), jnp.bfloat16),
+            pltpu.VMEM((groups, 2 * T * rows, mics_here), jnp.bfloat16),
             pltpu.VMEM((M, columns, mics_here), jnp.bfloat16),
             pltpu.VMEM((2, wb, 2, points, mics), jnp.bfloat16),
             pltpu.VMEM((2, wb * 2 * points, columns), jnp.float32),
@@ -355,9 +350,9 @@
             pltpu.VMEM((8, points), jnp.float32),
             DMA((slots,)),
             DMA(()),
-            DMA((steps, peers)),
-            DMA((steps, Z - 1)),
-            DMA((steps, M)),
+            DMA((groups, peers)),
+            DMA((groups, Z - 1)),
+            DMA((groups, M)),
             DMA((T,)),
             DMA((T,)),
             DMA((2,)),

time: 48.3 us -> 47.3 us (0.979)
  Pallas kernels: 46.9 us -> 45.8 us
    pallas_call x1, Pallas kernels: 46.9 us -> 45.8 us  [per_device(): pl.pallas_call(functools.partial(kernel, dims), out_shape=jax.ShapeDtypeS...]
where the time goes in v5:
time: 47.3 us; the launch traced here: 47.1 us
  Pallas kernels  45.8 us (97%)
  local copies, waits for them, and re-layouts  1.26 us (3%)
    pallas_call x1, Pallas kernels, per_device(): pl.pallas_call(functools.partial(kernel, dims), out_shape=jax.ShapeDtypeS...  45.8 us
    unnamed x1, local copies, waits for them, and re-layouts  1.26 us

profile of v5, /device:TPU:0, one launch (start us, length us, event | category | flops | bytes accessed | tf_op | source)
XLA Modules:
  0.0 47.1 jit_solution(14699431874067656355)
XLA Ops:
  0.0 45.8 %shard_map.37 = f32[4,128]{1,0:T(4,128)} custom-call(s32[16]{0:T(128)} %bins.1, bf16[8,512,4096]{2,1,0:T(8,128)(2,1)} %samples.1, s32[128,4096]{1,0:T(8,128)} %delays.1), custom_call_target="tpu_custom_call" | custom-call | flops 1073741824 | bytes 33554432 | tf_op jit(solution)/shard_map/pallas_call | solution.py:330
  45.8 1.3 %copy.5 = f32[4,128]{1,0:T(4,128)} copy(f32[4,128]{1,0:T(4,128)} %shard_map.37) | data formatting | bytes 4096

commit v6 on v3

--- a/solution.py
+++ b/solution.py
@@ -19,8 +19,8 @@
     return [float(c) for c in series.convert(kind=np.polynomial.Polynomial).coef]
 
 
-SIN_HALF = fit(lambda r: np.sin(np.pi * r) / r, 5)
-COS_HALF = fit(lambda r: np.cos(np.pi * r), 6)
+SIN_HALF = fit(lambda r: math.sqrt(2) * np.sin(np.pi * r) / r, 5)
+COS_HALF = fit(lambda r: math.sqrt(2) * np.cos(np.pi * r), 5)
 
 
 def horner(coefficients, y):
@@ -37,15 +37,14 @@
 def cos_turns(turns):
     r = fraction(turns)
     s = r * horner(SIN_HALF, r * r)
-    return 1.0 - (s + s) * s
+    return 1.0 - s * s
 
 
 def cos_sin_turns(turns):
     r = fraction(turns)
     y = r * r
     s = r * horner(SIN_HALF, y)
-    twice = s + s
-    return 1.0 - twice * s, twice * horner(COS_HALF, y)
+    return 1.0 - s * s, s * horner(COS_HALF, y)
 
 
 def kernel(dims, bins, samples, delays, out, table, held, delay, quarter, other_delay, spec, gath, steer, acc,
@@ -178,8 +177,8 @@
         slot = lax.rem(i, slots)
         fetch(i, slot).wait()
         block = held[slot].reshape(chunk_segs * group, length)
-        found = lax.dot_general(block, table[...], NT, preferred_element_type=jnp.float32)
-        found = [found[s * group:(s + 1) * group].T for s in range(chunk_segs)]
+        found = lax.dot_general(table[...], block, NT, preferred_element_type=jnp.float32)
+        found = [found[:, s * group:(s + 1) * group] for s in range(chunk_segs)]
         for worker in range(2 * T):
             lines = [f[worker * 2 * wb:(worker + 1) * 2 * wb] for f in found]
             spec[i, worker * rows:(worker + 1) * rows, :] = jnp.concatenate(lines, axis=0).astype(jnp.bfloat16)

time: 45.6 us -> 45.6 us (level)
  the two profiles are of different devices: /device:TPU:0 before, /device:TPU:1 now
where the time goes in v6:
time: 45.6 us; the launch traced here: 45.4 us
  Pallas kernels  44.2 us (97%)
  local copies, waits for them, and re-layouts  1.26 us (3%)
    pallas_call x1, Pallas kernels, per_device(): pl.pallas_call(functools.partial(kernel, dims), out_shape=jax.ShapeDtypeS...  44.2 us
    unnamed x1, local copies, waits for them, and re-layouts  1.26 us

profile of v6, /device:TPU:1, one launch (start us, length us, event | category | flops | bytes accessed | tf_op | source)
XLA Modules:
  0.0 45.4 jit_solution(12856687776522011726)
XLA Ops:
  0.0 44.2 %shard_map.37 = f32[4,128]{1,0:T(4,128)} custom-call(s32[16]{0:T(128)} %bins.1, bf16[8,512,4096]{2,1,0:T(8,128)(2,1)} %samples.1, s32[128,4096]{1,0:T(8,128)} %delays.1), custom_call_target="tpu_custom_call" | custom-call | flops 1073741824 | bytes 33554432 | tf_op jit(solution)/shard_map/pallas_call | solution.py:322
  44.2 1.3 %copy.5 = f32[4,128]{1,0:T(4,128)} copy(f32[4,128]{1,0:T(4,128)} %shard_map.37) | data formatting | bytes 4096

commit v7 on v6

--- a/solution.py
+++ b/solution.py
@@ -160,10 +160,15 @@
             src_ref=quarter, dst_ref=share_of(t), send_sem=quarter_send.at[0], recv_sem=quarter_recv.at[t],
             device_id={"tm": t, "mic": partner}, device_id_type=MESH)
 
+    beside = t + 1 - 2 * lax.rem(t, 2)
+    over = lax.rem(t + T // 2, T)
+    over_beside = lax.rem(beside + T // 2, T)
+
     def share_on(a):
+        owner, target = ((t, beside), (t, over), (over, beside))[a - 1]
         return pltpu.make_async_remote_copy(
-            src_ref=share_of(t), dst_ref=share_of(t), send_sem=quarter_send.at[a], recv_sem=quarter_recv.at[t],
-            device_id={"tm": lax.rem(t + a, T), "mic": m}, device_id_type=MESH)
+            src_ref=share_of(owner), dst_ref=share_of(owner), send_sem=quarter_send.at[a],
+            recv_sem=quarter_recv.at[owner], device_id={"tm": target, "mic": m}, device_id_type=MESH)
 
     def share_arrived(t2):
         pltpu.make_async_copy(share_of(t2), share_of(t2), quarter_recv.at[t2]).wait()
@@ -192,8 +197,8 @@
         @pl.when(i == 1)
         def _():
             share_arrived(t)
-            for a in range(1, T):
-                share_on(a).start()
+            share_on(2).start()
+            share_on(1).start()
 
         @pl.when(i >= 2)
         def _():
@@ -219,6 +224,12 @@
 
     def own_step(i, carry):
         steer_step(0, i)
+
+        @pl.when(i == pieces // 4)
+        def _():
+            share_arrived(over)
+            share_on(3).start()
+
         for turn, late in turn_of.items():
             @pl.when(i == turn)
             def _():
@@ -226,14 +237,22 @@
 
         return carry
 
-    def partner_step(i, carry):
-        steer_step(1, i)
-        return carry
-
     lax.fori_loop(0, pieces, own_step, 0)
-    for a in range(1, T):
-        share_arrived(lax.rem(t + a, T))
-    lax.fori_loop(0, pieces, partner_step, 0)
+    share_pieces = share // piece
+
+    def partner_steps(owner):
+        def one(n, carry):
+            steer_step(1, owner * share_pieces + n)
+            return carry
+
+        lax.fori_loop(0, share_pieces, one, 0)
+
+    partner_steps(t)
+    share_arrived(beside)
+    partner_steps(beside)
+    partner_steps(over)
+    share_arrived(over_beside)
+    partner_steps(over_beside)
 
     acc[...] = jnp.zeros_like(acc)
 
@@ -292,7 +311,7 @@
 
     lax.fori_loop(0, steps, drain, 0)
     give_share().wait_send()
-    for a in range(1, T):
+    for a in range(1, 4):
         share_on(a).wait_send()
     swap.wait()
     own = jnp.concatenate(own, axis=0)
@@ -345,7 +364,7 @@
             DMA((steps, peers)),
             DMA((steps, Z - 1)),
             DMA((steps, M)),
-            DMA((T,)),
+            DMA((4,)),
             DMA((T,)),
             DMA((2,)),
         ],

time: 45.6 us -> 44.4 us (0.974)
  the two profiles are of different devices: /device:TPU:1 before, /device:TPU:0 now
where the time goes in v7:
time: 44.4 us; the launch traced here: 44.2 us
  Pallas kernels  43 us (97%)
  local copies, waits for them, and re-layouts  1.26 us (3%)
    pallas_call x1, Pallas kernels, per_device(): pl.pallas_call(functools.partial(kernel, dims), out_shape=jax.ShapeDtypeS...  43 us
    unnamed x1, local copies, waits for them, and re-layouts  1.26 us

profile of v7, /device:TPU:0, one launch (start us, length us, event | category | flops | bytes accessed | tf_op | source)
XLA Modules:
  0.0 44.2 jit_solution(9258975578452256854)
XLA Ops:
  0.0 43.0 %shard_map.37 = f32[4,128]{1,0:T(4,128)} custom-call(s32[16]{0:T(128)} %bins.1, bf16[8,512,4096]{2,1,0:T(8,128)(2,1)} %samples.1, s32[128,4096]{1,0:T(8,128)} %delays.1), custom_call_target="tpu_custom_call" | custom-call | flops 1073741824 | bytes 33554432 | tf_op jit(solution)/shard_map/pallas_call | solution.py:341
  43.0 1.3 %copy.5 = f32[4,128]{1,0:T(4,128)} copy(f32[4,128]{1,0:T(4,128)} %shard_map.37) | data formatting | bytes 4096
